TPU v7x, 128 devices: a whole 4x4x4 slice. The times are simulated.
128 devices in a mesh: group: 4 (over z_lo, core), blk: 32 (over y, x, z_hi).
Axes of the slice: x: 4, y: 4, z: 4 (z_hi: 2, z_lo: 2; z = z_hi * 2 + z_lo), core: 2. Of those that a mesh axis runs over, the one named last changes fastest.
Arguments:
- query_hidden: bfloat16 [16384, 1024], P(('group', 'blk')), may hold values from -6 to 6
- passage_hidden: bfloat16 [32768, 1024], P(('group', 'blk')), may hold values from -6 to 6
- w_in: bfloat16 [1024, 4096], replicated, may hold values from -0.1875 to 0.1875
- w_out: bfloat16 [4096, 1024], replicated, may hold values from -0.09375 to 0.09375
- neg_unit: int32 [16384, 64], P(('group', 'blk')), may hold values from 0 to 255, all different within a row; in each aligned block of 128 rows (0 to 127, 128 to 255, ...) at most 48 rows name the same one
- neg_row: int32 [16384, 64], P(('group', 'blk')), may hold values from 0 to 127
- rank_order: int32 [16384, 64], P(('group', 'blk')), may hold values from 0 to 63, each once within a row
Outputs:
- contrast_loss: float32 [16384], P(('group', 'blk'))
- list_loss: float32 [16384], P(('group', 'blk'))
Inputs may be any that keep to these rules, and one draw needn't show every extreme that they name: `neg_unit`: each row names 64 different half-blocks; among the 128 rows of one device no half-block is named more than 48 times, and some half-block exactly 48 times. `rank_order`: each row holds every number of 0 to 63 once.
All inputs are finite; a program needn't handle non-finite values.
Results may differ from a plain program's by a relative error of at most 0.0011.
Values may be sent and summed in bfloat16 or wider, within the bound.
A program may use at most 192 MiB of HBM per device.

v0:
```python
import math

import jax
import jax.numpy as jnp
from jax import lax
from jax.sharding import PartitionSpec as P


def embed(hidden, w_in, w_out):
    act = jax.nn.gelu(
        jnp.dot(hidden, w_in, preferred_element_type=jnp.float32), approximate=True
    ).astype(jnp.bfloat16)
    return (
        hidden.astype(jnp.float32) + jnp.dot(act, w_out, preferred_element_type=jnp.float32)
    ).astype(jnp.bfloat16)


def merge_pair(first, second):
    top = jnp.maximum(first[0], second[0])
    return (top, first[1] * jnp.exp(first[0] - top) + second[1] * jnp.exp(second[0] - top))


def listwise(hard, rank_order):
    slots = jnp.arange(hard.shape[1], dtype=jnp.int32)
    ordered = jnp.sum(
        jnp.where(rank_order[:, :, None] == slots[None, None, :], hard[:, None, :], 0.0), axis=2
    )
    tops, totals = lax.associative_scan(
        merge_pair, (ordered, jnp.ones_like(ordered)), reverse=True, axis=1
    )
    return jnp.mean(tops + jnp.log(totals) - ordered, axis=1)


def build_requests(hits, earlier, local_row, bucket):
    named = jnp.any(hits, axis=1)
    row_table = jnp.sum(jnp.where(hits, local_row[:, :, None], 0), axis=1)
    places = jnp.arange(bucket, dtype=jnp.int32)
    select = named[:, :, None] & (earlier[:, :, None] == places[None, None, :])
    return jnp.sum(jnp.where(select, row_table[:, :, None], 0), axis=0)


def select_hard(scores, earlier, hits):
    places = jnp.arange(scores.shape[2], dtype=jnp.int32)
    per_unit = jnp.sum(jnp.where(earlier[:, :, None] == places[None, None, :], scores, 0.0), axis=2)
    return jnp.sum(jnp.where(hits, per_unit[:, None, :], 0.0), axis=2)


def body(query_hidden, passage_hidden, w_in, w_out, neg_unit, neg_row, rank_order):
    query_emb = embed(query_hidden, w_in, w_out)
    passage_emb = embed(passage_hidden, w_in, w_out)
    queries, width = query_emb.shape
    passages = passage_emb.shape[0]
    negatives = neg_unit.shape[1]
    groups = lax.axis_size("group")
    blocks = lax.axis_size("blk")
    devices = groups * blocks
    units = 2 * devices
    bucket = min(queries, 3 * queries * negatives // (4 * devices))
    scale = 1.0 / math.sqrt(width)
    unit_ids = jnp.arange(units, dtype=jnp.int32)
    hits = neg_unit[:, :, None] == unit_ids[None, None, :]
    named = jnp.any(hits, axis=1).astype(jnp.bfloat16)
    row_ids = jnp.arange(queries, dtype=jnp.int32)
    lower = (row_ids[:, None] > row_ids[None, :]).astype(jnp.bfloat16)
    earlier = jnp.dot(lower, named, preferred_element_type=jnp.float32).astype(jnp.int32)
    local_row = neg_unit % 2 * (passages // 2) + neg_row
    requests = build_requests(hits, earlier, local_row, bucket).reshape(devices, 2 * bucket)
    start_carry = (jnp.full((queries,), -1e30, jnp.float32), jnp.zeros((queries,), jnp.float32))
    top = start_carry[0]
    tile = (
        jnp.einsum(
            "qd,pd->qp",
            query_emb,
            lax.all_gather(passage_emb, "blk", axis=0, tiled=True),
            preferred_element_type=jnp.float32,
        )
        * scale
    )
    new_top = jnp.maximum(top, jnp.max(tile, axis=1))
    total = jnp.sum(jnp.exp(tile - new_top[:, None]), axis=1)
    cycle_top, cycle_total = (new_top, total)
    fetched = lax.all_to_all(
        jnp.take(
            passage_emb,
            lax.all_to_all(requests, ("group", "blk"), split_axis=0, concat_axis=0, tiled=True),
            axis=0,
        ),
        ("group", "blk"),
        split_axis=0,
        concat_axis=0,
        tiled=True,
    )
    flat_rows = fetched.reshape(units * bucket, width)
    scores = jnp.dot(query_emb, flat_rows.T, preferred_element_type=jnp.float32) * scale
    hard = select_hard(scores.reshape(queries, units, bucket), earlier, hits)
    pos = (
        jnp.sum(query_emb.astype(jnp.float32) * passage_emb[:queries].astype(jnp.float32), axis=1)
        * scale
    )
    top = jnp.maximum(cycle_top, jnp.max(hard, axis=1))
    total = cycle_total * jnp.exp(cycle_top - top) + jnp.sum(jnp.exp(hard - top[:, None]), axis=1)
    contrast_loss = jnp.log(total) + top - pos
    return (contrast_loss, listwise(hard, rank_order))


def solution(mesh):
    return jax.shard_map(
        body,
        mesh=mesh,
        in_specs=(
            P(("group", "blk"), None),
            P(("group", "blk"), None),
            P(),
            P(),
            P(("group", "blk"), None),
            P(("group", "blk"), None),
            P(("group", "blk"), None),
        ),
        out_specs=(P(("group", "blk")), P(("group", "blk"))),
        check_vma=False,
    )
```

profile of v0, /device:TPU:101, one launch (start us, length us, event | category | flops | bytes accessed | tf_op | source)
XLA Modules:
  0.0 633.3 jit_solution(153857754415144596)
XLA Ops:
  7.2 0.8 copy.35
  8.0 2.5 fusion
  10.5 0.2 convolution_convert_fusion
  10.7 0.1 copy.37
  10.8 0.1 copy.36
  10.9 0.8 fusion.38
  11.7 0.1 copy.38
  11.8 2.8 select_reduce_fusion.1
  14.6 0.1 copy.39
  14.7 4.4 select_reduce_fusion.3
  19.1 0.7 all_to_all.13
  19.8 10.1 %all-to-all-start = ((s32[128,1,96]{2,1,0:T(1,128)}), s32[128,1,96]{2,1,0:T(1,128)S(1)}, u32[]{:S(2)}, u32[]{:S(2)}) async-start(s32[128,1,96]{2,1,0:T(1,128)} %bitcast), calls=%async_computation | async-start | bytes 131072 | tf_op jit(solution)/shard_map/all_to_all | solution.py:85
  30.0 0.0 all-gather.2.cloned.1.call-start
  30.0 11.6 %fusion.27 = bf16[256,1024]{1,0:T(8,128)(2,1)} fusion(bf16[4096,1024]{1,0:T(8,128)(2,1)} %param.10, bf16[256,1024]{1,0:T(8,128)(2,1)} %param.8, bf16[1024,4096]{1,0:T(8,128)(2,1)} %param.9), kind=kOutput, calls=%fused_computation.39 | convolution fusion | flops 4305190912 | bytes 17825792 | tf_op jit(solution)/shard_map/dot_general | solution.py:14
  41.6 0.0 copy-start
  41.6 0.0 all-gather.2.cloned.1.call-update
  41.7 0.0 all-to-all-done
  41.7 0.1 reshape.68
  41.8 0.9 copy-done
  42.7 52.6 %gather_fusion = bf16[12288,1024]{1,0:T(8,128)(2,1)} fusion(bf16[256,1024]{1,0:T(8,128)(2,1)S(1)} %copy-done, s32[12288]{0:T(1024)S(1)} %broadcast_clamp_fusion), kind=kCustom, calls=%fused_computation | custom fusion | bytes 50380800 | tf_op jit(solution)/shard_map/jit(_take)/gather | solution.py:83
  95.3 21.8 %broadcast_select_fusion = bf16[128,96,1024]{2,1,0:T(8,128)(2,1)} fusion(bf16[128,96,1024]{2,1,0:T(8,128)(2,1)} %bitcast.19, pred[128,96]{1,0:T(8,128)(4,1)S(1)} %compare_and_fusion), kind=kLoop, calls=%fused_computation.1 | loop fusion | flops 12582912 | bytes 50343936 | tf_op jit(solution)/shard_map/jit(_take)/select_n | solution.py:83
  117.2 0.0 copy-start.2
  117.2 10.2 %all-to-all-start.1 = ((bf16[128,96,1024]{2,1,0:T(8,128)(2,1)}), bf16[128,96,1024]{2,1,0:T(8,128)(2,1)}, u32[]{:S(2)}, u32[]{:S(2)}) async-start(bf16[128,96,1024]{2,1,0:T(8,128)(2,1)} %broadcast_select_fusion), calls=%async_computation.1 | async-start | bytes 50331648 | tf_op jit(solution)/shard_map/all_to_all | solution.py:82
  127.3 0.0 copy-done.2
  127.4 8.8 %multiply_reduce_fusion = (f32[128]{0:T(128)S(1)}, bf16[128,1024]{1,0:T(8,128)(2,1)S(1)}) fusion(bf16[256,1024]{1,0:T(8,128)(2,1)S(1)} %copy-done, bf16[4096,1024]{1,0:T(8,128)(2,1)} %param.10, bf16[128,1024]{1,0:T(8,128)(2,1)S(1)} %copy-done.2, bf16[1024,4096]{1,0:T(8,128)(2,1)} %param.9), kind=kOutput, calls=%fused_computation.47 | convolution fusion | flops 2153119744 | bytes 17826304 | tf_op jit(solution)/shard_map/dot_general | solution.py:14
  136.1 442.4 %all-to-all-done.1 = bf16[128,96,1024]{2,1,0:T(8,128)(2,1)} async-done(((bf16[128,96,1024]{2,1,0:T(8,128)(2,1)}), bf16[128,96,1024]{2,1,0:T(8,128)(2,1)}, u32[]{:S(2)}, u32[]{:S(2)}) %all-to-all-start.1) | async-done | bytes 25165856 | tf_op jit(solution)/shard_map/all_to_all | solution.py:82
  578.5 14.7 %convolution_multiply_fusion = f32[128,12288]{1,0:T(8,128)} fusion(bf16[128,1024]{1,0:T(8,128)(2,1)S(1)} %get-tuple-element.31, bf16[12288,1024]{1,0:T(8,128)(2,1)} %bitcast.4), kind=kOutput, calls=%fused_computation.2 | convolution fusion | flops 3222798336 | bytes 31719424 | tf_op jit(solution)/shard_map/dot_general | solution.py:94
  593.2 6.6 %copy.41 = f32[128,12288]{0,1:T(8,128)} copy(f32[128,12288]{1,0:T(8,128)} %convolution_multiply_fusion) | data formatting | bytes 12582912 | tf_op jit(solution)/shard_map/mul | solution.py:94
  599.8 0.0 copy-start.1
  599.8 4.2 select_reduce_fusion.2
  604.0 0.1 copy.42
  604.1 2.9 select_reduce_fusion
  607.1 0.1 copy.43
  607.1 0.0 copy-done.1
  607.2 0.5 select_reduce_fusion.4
  608.9 0.1 reduce_max.19
  609.1 0.5 broadcast_multiply_fusion
  609.6 0.0 all-gather.2.cloned.1.call-done
  609.6 13.4 %fusion.54 = (f32[128]{0:T(128)S(1)}, f32[128,8192]{1,0:T(8,128)}) fusion(bf16[128,1024]{1,0:T(8,128)(2,1)S(1)} %get-tuple-element.31, bf16[8192,1024]{1,0:T(8,128)(2,1)} %all-gather.2.cloned.1.call-done), kind=kOutput, calls=%fused_computation.105 | convolution fusion | flops 2149580800 | bytes 21234176 | tf_op jit(solution)/shard_map/qd,pd->qp/dot_general | solution.py:71
  623.0 2.9 exponential_reduce_fusion
  625.9 0.5 multiply_subtract_fusion
  (95 shorter events, 1.0 us)
Async XLA Ops:
  19.8 21.8 %all-to-all-start = ((s32[128,1,96]{2,1,0:T(1,128)}), s32[128,1,96]{2,1,0:T(1,128)S(1)}, u32[]{:S(2)}, u32[]{:S(2)}) async-start(s32[128,1,96]{2,1,0:T(1,128)} %bitcast), calls=%async_computation | async-start | bytes 131072 | tf_op jit(solution)/shard_map/all_to_all | solution.py:85
  30.0 579.6 %all-gather.2.cloned.1.call-start = ((), (), s32[]{:S(2)}) async-start(), calls=%async_computation.2 | async-start | bytes 17301504 | tf_op jit(solution)/shard_map/all_gather | solution.py:74
  41.6 1.0 copy-start
  117.2 10.2 %copy-start.2 = (bf16[128,1024]{1,0:T(8,128)(2,1)S(1)}, bf16[128,1024]{1,0:T(8,128)(2,1)}, u32[]{:S(2)}) copy-start(bf16[128,1024]{1,0:T(8,128)(2,1)} %param.7) | copy-start | bytes 786436
  117.2 461.3 %all-to-all-start.1 = ((bf16[128,96,1024]{2,1,0:T(8,128)(2,1)}), bf16[128,96,1024]{2,1,0:T(8,128)(2,1)}, u32[]{:S(2)}, u32[]{:S(2)}) async-start(bf16[128,96,1024]{2,1,0:T(8,128)(2,1)} %broadcast_select_fusion), calls=%async_computation.1 | async-start | bytes 50331648 | tf_op jit(solution)/shard_map/all_to_all | solution.py:82
  599.8 7.3 %copy-start.1 = (s32[128,64]{0,1:T(8,128)S(1)}, s32[128,64]{0,1:T(8,128)}, u32[]{:S(2)}) copy-start(s32[128,64]{0,1:T(8,128)} %param.13) | copy-start | bytes 98308
Sparse Core Ops, SparseCore 0:
  41.8 464.9 all-gather.1
where the time goes:
time: 634 us; the launch traced here: 633 us
  waiting for transfers between devices  442 us (70%)
  local copies, waits for them, and re-layouts  63 us (10%)
  matrix products  48.6 us (8%)
  other arithmetic  44.4 us (7%)
  starting transfers between devices  20.3 us (3%)
  between operations  14.6 us (2%)
    all_to_all x1, waiting for transfers between devices, body(): lax.all_to_all(jnp.take(passage_emb, lax.all_to_all(requests, ('group', '...  442 us
    gather x1, local copies, waits for them, and re-layouts, body(): jnp.take(passage_emb, lax.all_to_all(requests, ('group', 'blk'), split_ax...  52.6 us
    select_n x2, other arithmetic, body(): jnp.take(passage_emb, lax.all_to_all(requests, ('group', 'blk'), split_ax...  21.9 us
    dot_general x2, matrix products, embed(): jnp.dot(act, w_out, preferred_element_type=jnp.float32)  20.4 us
    dot_general x1, matrix products, body(): jnp.dot(query_emb, flat_rows.T, preferred_element_type=jnp.float32) * scale  14.7 us
    dot_general x1, matrix products, body(): jnp.einsum('qd,pd->qp', query_emb, lax.all_gather(passage_emb, 'blk', axi...  13.4 us
  transfers between devices with their start and end apart: 3, of which 1 were waited for; matrix products, arithmetic and copies ran while one was open for 20% of the time, Pallas kernels for 0%

commit v1 on v0

v1 whole, which is shorter than its diff:
```python
import math

import jax
import jax.numpy as jnp
from jax import lax
from jax.experimental import pallas as pl
from jax.experimental.pallas import tpu as pltpu
from jax.sharding import PartitionSpec as P

MESH = pl.DeviceIdType.MESH
BF16 = jnp.bfloat16
F32 = jnp.float32
I32 = jnp.int32
NEG_BIG = -1e30


def kernel(
    qh, ph, nu, nr, ro, wi_hbm, wo_hbm,
    contrast_out, list_out,
    wi, wo, x, act, qbuf, pbuf, ncode, nrow, order, code, tsend, tin, hsend, hin,
    wsem, xsem, send, recv, rqs, rqr, rts, rtr,
):
    width = x.shape[1]
    queries = 128
    passages = 256
    scale = 1.0 / math.sqrt(width)

    g = lax.axis_index("group")
    b = lax.axis_index("blk")
    core = g % 2
    zl = g // 2
    zh = b % 2
    px = (b // 2) % 4
    py = b // 8
    z = zh * 2 + zl
    r1 = px * (1 - core) + py * core
    r2 = py * (1 - core) + px * core
    me = r2 * 4 + r1

    def plane_dev(a1, a2):
        ax = a1 * (1 - core) + a2 * core
        ay = a2 * (1 - core) + a1 * core
        return (g, ay * 8 + ax * 2 + zh)

    def column_dev(az, ac):
        return ((az % 2) * 2 + ac, py * 8 + px * 2 + az // 2)

    def up(v, d):
        return (v + d) % 4

    nchunk = 4
    ff_c = wi.shape[1] // nchunk
    n_c = wo.shape[1] // nchunk

    def wi_copy(i):
        s = pl.ds(i * ff_c, ff_c)
        return pltpu.make_async_copy(wi_hbm.at[:, s], wi.at[:, s], wsem.at[i])

    def wo_copy(i):
        s = pl.ds(i * n_c, n_c)
        return pltpu.make_async_copy(wo_hbm.at[:, s], wo.at[:, s], wsem.at[nchunk + i])

    xq = pltpu.make_async_copy(qh, x.at[pl.ds(0, queries)], xsem.at[0])
    xp = pltpu.make_async_copy(ph, x.at[pl.ds(queries, passages)], xsem.at[1])
    xq.start()
    xp.start()
    for i in range(nchunk):
        wi_copy(i).start()

    barrier = pltpu.get_barrier_semaphore()

    def greet(d, _):
        pl.semaphore_signal(
            barrier, inc=1, device_id=plane_dev(up(r1, d % 4), up(r2, d // 4)), device_id_type=MESH
        )
        return 0

    lax.fori_loop(1, 16, greet, 0)
    for dev in (column_dev(z, 1 - core), column_dev(up(z, 1), core), column_dev(up(z, 3), core)):
        pl.semaphore_signal(barrier, inc=1, device_id=dev, device_id_type=MESH)

    unit = nu[...]
    vx = (unit >> 2) & 3
    vy = (unit >> 4) & 3
    v1 = vx * (1 - core) + vy * core
    v2 = vy * (1 - core) + vx * core
    within = (((unit >> 1) & 1) << 3) | (((unit >> 7) & 1) << 2) | (((unit >> 6) & 1) << 1) | (unit & 1)
    ncode[...] = (v2 << 6) | (v1 << 4) | within
    nrow[...] = nr[...]
    order[...] = ro[...]

    def build(i, _):
        ids = i * 64 + lax.broadcasted_iota(I32, (64, queries), 0)
        acc = jnp.full((64, queries), -1, I32)
        for k in range(64):
            acc = jnp.where(ids == ncode[k : k + 1, :], nrow[k : k + 1, :], acc)
        tsend[pl.ds(i * 4, 4)] = acc.reshape(4, 16, queries)
        return 0

    lax.fori_loop(0, 4, build, 0)
    acc = jnp.zeros((64, queries), I32)
    for k in range(64):
        acc = jnp.where(order[...] == k, ncode[k : k + 1, :], acc)
    code[...] = acc

    xq.wait()
    xp.wait()
    for c in range(nchunk):
        wi_copy(c).wait()
        wo_copy(c).start()

        def up_proj(j, _, c=c):
            s = pl.ds(pl.multiple_of(c * ff_c + j * 256, 256), 256)
            h = jnp.dot(x[...], wi[:, s], preferred_element_type=F32)
            act[:, s] = jax.nn.gelu(h, approximate=True).astype(BF16)
            return 0

        lax.fori_loop(0, ff_c // 256, up_proj, 0)

    pl.semaphore_wait(barrier, 18)

    def request(d):
        a1, a2 = up(r1, d % 4), up(r2, d // 4)
        return pltpu.make_async_remote_copy(
            src_ref=tsend.at[a2 * 4 + a1], dst_ref=tin.at[me],
            send_sem=rqs.at[d], recv_sem=rqr.at[d],
            device_id=plane_dev(a1, a2), device_id_type=MESH,
        )

    def request_start(d, _):
        request(d).start()
        return 0

    lax.fori_loop(1, 16, request_start, 0)
    tin[me] = tsend[me]

    own_q = pl.ds(pl.multiple_of(r1 * 128, 128), 128)
    own_p = z * 2 + core
    sent = []

    def remote(src, dst, idx, dev):
        cp = pltpu.make_async_remote_copy(
            src_ref=src, dst_ref=dst, send_sem=send.at[idx], recv_sem=recv.at[idx],
            device_id=dev, device_id_type=MESH,
        )
        return cp

    def go(src, idx, dev):
        cp = remote(src, src, idx, dev)
        cp.start()
        sent.append(cp)

    def arrived(ref, idx):
        remote(ref, ref, idx, (g, b)).wait_recv()

    for c in range(nchunk):
        wo_copy(c).wait()
        s = pl.ds(c * n_c, n_c)
        o = jnp.dot(act[0:queries, :], wo[:, s], preferred_element_type=F32)
        qbuf[r2, own_q, s] = (x[0:queries, s].astype(F32) + o).astype(BF16)

    def piece(a2, a1, lo=0, n=128):
        return qbuf.at[a2, pl.ds(pl.multiple_of(a1 * 128 + lo, 64), n)]

    r1p, r1m, r1f = up(r1, 1), up(r1, 3), up(r1, 2)
    r2p, r2m, r2f = up(r2, 1), up(r2, 3), up(r2, 2)
    dev1p, dev1m = plane_dev(r1p, r2), plane_dev(r1m, r2)
    dev2p, dev2m = plane_dev(r1, r2p), plane_dev(r1, r2m)
    cols = (r1, r1m, r1p, r1f)

    def spread(i):
        go(piece(r2, cols[i]), 4 + 2 * i, dev2p)
        go(piece(r2, cols[i]), 5 + 2 * i, dev2m)

    go(piece(r2, r1), 0, dev1p)
    go(piece(r2, r1), 1, dev1m)
    spread_own = spread
    spread_own(0)

    def down_proj(j, _):
        s = pl.ds(pl.multiple_of(j * n_c, n_c), n_c)
        o = jnp.dot(act[queries:, :], wo[:, s], preferred_element_type=F32)
        pbuf[own_p, :, s] = (x[queries:, s].astype(F32) + o).astype(BF16)
        return 0

    lax.fori_loop(0, nchunk, down_proj, 0)

    def half(az, ac, h):
        return pbuf.at[az * 2 + ac, pl.ds(h * 128, 128)]

    zp, zm, zf = up(z, 1), up(z, 3), up(z, 2)
    sib = column_dev(z, 1 - core)
    devzp, devzm = column_dev(zp, core), column_dev(zm, core)
    for h in range(2):
        go(half(z, core, h), 16 + h, sib)
        go(half(z, core, h), 18 + h, devzp)
        go(half(z, core, h), 20 + h, devzm)

    rows = lax.broadcasted_iota(I32, (128, 128), 0)
    lanes = lax.broadcasted_iota(I32, (128, 128), 1)
    dims = (((1,), (1,)), ((), ()))

    s_own = lax.dot_general(pbuf[own_p, 0:128, :], qbuf[r2, own_q, :], dims, preferred_element_type=F32)
    pos = jnp.sum(jnp.where(rows == lanes, s_own, 0.0), axis=0, keepdims=True) * scale

    def task(a2, pb, slot):
        s = lax.dot_general(pbuf[pb], qbuf[a2], dims, preferred_element_type=F32)
        for h in range(2):
            for i in range(4):
                part = s[h * 128 : (h + 1) * 128, i * 128 : (i + 1) * 128]
                want = tin[a2 * 4 + i, pl.ds(pb * 2 + h, 1), :]
                hsend[a2 * 4 + i, pl.ds(pb * 2 + h, 1), :] = jnp.sum(
                    jnp.where(rows == want, part, 0.0), axis=0, keepdims=True
                )
        if slot is not None:
            top = jnp.max(s, axis=0, keepdims=True)
            total = jnp.sum(jnp.exp((s - top) * scale), axis=0, keepdims=True)
            for i in range(4):
                w = slice(i * 128, (i + 1) * 128)
                hsend[a2 * 4 + i, 16 + 2 * slot : 17 + 2 * slot, :] = top[:, w]
                hsend[a2 * 4 + i, 17 + 2 * slot : 18 + 2 * slot, :] = total[:, w]

    def tasks(lo, hi, block, slot):
        def step(i, _):
            task(up(r2, i), block, slot)
            return 0

        lax.fori_loop(lo, hi, step, 0)

    arrived(piece(r2, r1m), 0)
    go(piece(r2, r1m, 0, 64), 2, dev1p)
    spread(1)
    arrived(piece(r2, r1p), 1)
    go(piece(r2, r1p, 64, 64), 3, dev1m)
    spread(2)
    arrived(piece(r2m, r1), 4)
    go(piece(r2m, r1), 12, dev2p)
    arrived(piece(r2p, r1), 5)
    arrived(piece(r2, r1f, 0, 64), 2)
    arrived(piece(r2, r1f, 64, 64), 3)
    spread(3)

    def request_wait(d, _):
        request(d).wait_recv()
        return 0

    lax.fori_loop(1, 16, request_wait, 0)

    tasks(0, 1, own_p, 0)
    arrived(half(z, 1 - core, 0), 16)
    arrived(half(z, 1 - core, 1), 17)
    tasks(0, 1, z * 2 + 1 - core, None)

    for h in range(2):
        arrived(half(zm, core, h), 18 + h)
        if h == 0:
            go(half(zm, core, 0), 22, devzp)
        go(half(zm, core, h), 24 + h, sib)
        arrived(half(zp, core, h), 20 + h)
        if h == 1:
            go(half(zp, core, 1), 23, devzm)
        go(half(zp, core, h), 26 + h, sib)
    arrived(piece(r2p, r1m), 7)
    go(piece(r2p, r1m), 13, dev2m)
    arrived(piece(r2p, r1p), 9)
    go(piece(r2p, r1p), 14, dev2m)
    arrived(piece(r2m, r1m), 6)
    arrived(piece(r2m, r1p), 8)
    arrived(piece(r2m, r1f), 10)
    go(piece(r2m, r1f), 15, dev2p)
    arrived(piece(r2p, r1f), 11)

    tasks(0, 1, zm * 2 + core, None)
    tasks(0, 1, zp * 2 + core, None)
    for h in range(2):
        arrived(half(zf, core, h), 22 + h)
        go(half(zf, core, h), 28 + h, sib)
    for h in range(2):
        arrived(half(zm, 1 - core, h), 24 + h)
        arrived(half(zp, 1 - core, h), 26 + h)
    for i in (1, 3):
        for blk, slot in ((own_p, 0), (z * 2 + 1 - core, None), (zm * 2 + core, None), (zp * 2 + core, None)):
            tasks(i, i + 1, blk, slot)
    tasks(0, 1, zf * 2 + core, 1)
    for i in (0, 1, 3):
        for blk in (zm * 2 + 1 - core, zp * 2 + 1 - core):
            tasks(i, i + 1, blk, None)
    for i in range(4):
        arrived(piece(r2f, cols[i]), 12 + i)
    for blk, slot in (
        (own_p, 0), (z * 2 + 1 - core, None), (zm * 2 + core, None), (zp * 2 + core, None),
        (zm * 2 + 1 - core, None), (zp * 2 + 1 - core, None),
    ):
        tasks(2, 3, blk, slot)
    tasks(1, 4, zf * 2 + core, 1)
    for h in range(2):
        arrived(half(zf, 1 - core, h), 28 + h)
    tasks(0, 4, zf * 2 + 1 - core, None)

    def answer(d):
        a1, a2 = up(r1, d % 4), up(r2, d // 4)
        return pltpu.make_async_remote_copy(
            src_ref=hsend.at[a2 * 4 + a1], dst_ref=hin.at[me],
            send_sem=rts.at[d], recv_sem=rtr.at[d],
            device_id=plane_dev(a1, a2), device_id_type=MESH,
        )

    def answer_start(d, _):
        answer(d).start()
        return 0

    def answer_wait(d, _):
        answer(d).wait_recv()
        return 0

    lax.fori_loop(1, 16, answer_start, 0)
    hin[me] = hsend[me]
    lax.fori_loop(1, 16, answer_wait, 0)

    def collect(s, ordered):
        for j in range(16):
            ordered = jnp.where(code[...] == s * 16 + j, hin[s, j : j + 1, :], ordered)
        return ordered

    ordered = lax.fori_loop(0, 16, collect, jnp.zeros((64, queries), F32)) * scale

    tops = jnp.concatenate([hin[:, 16, :], hin[:, 18, :]], axis=0) * scale
    totals = jnp.concatenate([hin[:, 17, :], hin[:, 19, :]], axis=0)
    top = jnp.maximum(jnp.max(tops, axis=0, keepdims=True), jnp.max(ordered, axis=0, keepdims=True))
    total = jnp.sum(totals * jnp.exp(tops - top), axis=0, keepdims=True)
    total = total + jnp.sum(jnp.exp(ordered - top), axis=0, keepdims=True)
    contrast_out[...] = jnp.log(total) + top - pos

    m, t = ordered, jnp.ones_like(ordered)
    for sh in (1, 2, 4, 8, 16, 32):
        m2 = jnp.concatenate([m[sh:], jnp.full((sh, queries), NEG_BIG, F32)], axis=0)
        t2 = jnp.concatenate([t[sh:], jnp.zeros((sh, queries), F32)], axis=0)
        mm = jnp.maximum(m, m2)
        t = t * jnp.exp(m - mm) + t2 * jnp.exp(m2 - mm)
        m = mm
    list_out[...] = jnp.mean(m + jnp.log(t) - ordered, axis=0, keepdims=True)

    for cp in sent:
        cp.wait_send()

    def drain(d, _):
        request(d).wait_send()
        answer(d).wait_send()
        return 0

    lax.fori_loop(1, 16, drain, 0)


def body(query_hidden, passage_hidden, w_in, w_out, neg_unit, neg_row, rank_order):
    width, ff = w_in.shape
    anyspec = pl.BlockSpec(memory_space=pl.ANY)
    vmem = pl.BlockSpec(memory_space=pltpu.VMEM)
    dma = pltpu.SemaphoreType.DMA
    contrast, listwise = pl.pallas_call(
        kernel,
        out_shape=(jax.ShapeDtypeStruct((1, 128), F32), jax.ShapeDtypeStruct((1, 128), F32)),
        in_specs=[anyspec, anyspec, vmem, vmem, vmem, anyspec, anyspec],
        out_specs=(vmem, vmem),
        scratch_shapes=[
            pltpu.VMEM((width, ff), BF16),
            pltpu.VMEM((ff, width), BF16),
            pltpu.VMEM((384, width), BF16),
            pltpu.VMEM((384, ff), BF16),
            pltpu.VMEM((4, 512, width), BF16),
            pltpu.VMEM((8, 256, width), BF16),
            pltpu.VMEM((64, 128), I32),
            pltpu.VMEM((64, 128), I32),
            pltpu.VMEM((64, 128), I32),
            pltpu.VMEM((64, 128), I32),
            pltpu.VMEM((16, 16, 128), I32),
            pltpu.VMEM((16, 16, 128), I32),
            pltpu.VMEM((16, 24, 128), F32),
            pltpu.VMEM((16, 24, 128), F32),
            dma((8,)),
            dma((2,)),
            dma((30,)),
            dma((30,)),
            dma((16,)),
            dma((16,)),
            dma((16,)),
            dma((16,)),
        ],
        compiler_params=pltpu.CompilerParams(
            collective_id=0, has_side_effects=True, vmem_limit_bytes=56 * 1024 * 1024
        ),
        name="distill",
    )(query_hidden, passage_hidden, neg_unit.T, neg_row.T, rank_order.T, w_in, w_out)
    return contrast.reshape(128), listwise.reshape(128)


def solution(mesh):
    split = P(("group", "blk"), None)
    return jax.shard_map(
        body,
        mesh=mesh,
        in_specs=(split, split, P(), P(), split, split, split),
        out_specs=(P(("group", "blk")), P(("group", "blk"))),
        check_vma=False,
    )
```

time: 634 us -> 63 us (0.10)
  the two profiles are of different devices: /device:TPU:101 before, /device:TPU:1 now
where the time goes in v1:
time: 63 us; the launch traced here: 62.4 us
  Pallas kernels  59.6 us (95%)
  local copies, waits for them, and re-layouts  2.25 us (4%)
  between operations  0.64 us (1%)
    pallas_call x1, Pallas kernels, body(): pl.pallas_call(kernel, out_shape=(jax.ShapeDtypeStruct((1, 128), F32), ja...  59.6 us
    unnamed x2, local copies, waits for them, and re-layouts  2.25 us

profile of v1, /device:TPU:1, one launch (start us, length us, event | category | flops | bytes accessed | tf_op | source)
XLA Modules:
  0.0 62.4 jit_solution(13822763201074083224)
XLA Ops:
  0.6 59.6 %distill.1 = (f32[1,128]{1,0:T(1,128)}, f32[1,128]{1,0:T(1,128)}) custom-call(bf16[128,1024]{1,0:T(8,128)(2,1)} %qh.1, bf16[256,1024]{1,0:T(8,128)(2,1)} %ph.1, s32[64,128]{1,0:T(8,128)} %bitcast.5, s32[64,128]{1,0:T(8,128)} %bitcast.6, s32[64,128]{1,0:T(8,128)} %bitcast.7, bf16[1024,4096]{1,0:T(8,128)(2,1)} %wi_hbm.1, bf16[4096,1024]{1,0:T(8,128)(2,1)} %wo_hbm.1), custom_call_target="tpu_custom_call" | custom-call | tf_op jit(solution)/shard_map/distill/pallas_call | solution.py:359
  60.2 1.1 %copy.11 = f32[128]{0:T(128)} copy(f32[128]{0:T(128)} %bitcast.9) | data formatting | bytes 1024
  61.3 1.1 %copy.12 = f32[128]{0:T(128)} copy(f32[128]{0:T(128)} %bitcast.8) | data formatting | bytes 1024

commit v2 on v0

v2 whole, which is shorter than its diff:
```python
import math

import jax
import jax.numpy as jnp
from jax import lax
from jax.experimental import pallas as pl
from jax.experimental.pallas import tpu as pltpu
from jax.sharding import PartitionSpec as P

MESH = pl.DeviceIdType.MESH
BF16 = jnp.bfloat16
F32 = jnp.float32
I32 = jnp.int32
NEG_BIG = -1e30


def kernel(
    qh, ph, nu, nr, ro, wi_hbm, wo_hbm,
    contrast_out, list_out,
    wi, wo, x, act, qbuf, pbuf, ncode, code, tsend, tin, hsend, hin,
    wsem, xsem, send, recv, rqs, rqr, rts, rtr,
):
    width = x.shape[1]
    queries = 128
    passages = 256
    scale = 1.0 / math.sqrt(width)

    g = lax.axis_index("group")
    b = lax.axis_index("blk")
    core = g % 2
    zl = g // 2
    zh = b % 2
    px = (b // 2) % 4
    py = b // 8
    z = zh * 2 + zl
    r1 = px * (1 - core) + py * core
    r2 = py * (1 - core) + px * core

    def plane_dev(d1, d2):
        a1, a2 = (r1 + d1) % 4, (r2 + d2) % 4
        ax = a1 * (1 - core) + a2 * core
        ay = a2 * (1 - core) + a1 * core
        return (g, ay * 8 + ax * 2 + zh)

    def column_dev(dz, dc):
        az, ac = (z + dz) % 4, (core + dc) % 2
        return ((az % 2) * 2 + ac, py * 8 + px * 2 + az // 2)

    others = [(p % 4, p // 4) for p in range(1, 16)]

    n_in, n_out = 4, 2
    c_in, c_out = wi.shape[1] // n_in, wo.shape[1] // n_out

    def wi_copy(i):
        s = pl.ds(i * c_in, c_in)
        return pltpu.make_async_copy(wi_hbm.at[:, s], wi.at[:, s], wsem.at[i])

    def wo_copy(i):
        s = pl.ds(i * c_out, c_out)
        return pltpu.make_async_copy(wo_hbm.at[:, s], wo.at[:, s], wsem.at[n_in + i])

    xq = pltpu.make_async_copy(qh, x.at[pl.ds(0, queries)], xsem.at[0])
    xp = pltpu.make_async_copy(ph, x.at[pl.ds(queries, passages)], xsem.at[1])
    xq.start()
    xp.start()
    for i in range(n_in):
        wi_copy(i).start()

    barrier = pltpu.get_barrier_semaphore()
    sib, dev_zp, dev_zm = column_dev(0, 1), column_dev(1, 0), column_dev(3, 0)
    for dev in [plane_dev(d1, d2) for d1, d2 in others] + [sib, dev_zp, dev_zm]:
        pl.semaphore_signal(barrier, inc=1, device_id=dev, device_id_type=MESH)

    unit = nu[...]
    vx = (unit >> 2) & 3
    vy = (unit >> 4) & 3
    d1 = (vx * (1 - core) + vy * core - r1) & 3
    d2 = (vy * (1 - core) + vx * core - r2) & 3
    dz = (((unit >> 1) & 1) * 2 + ((unit >> 7) & 1) - z) & 3
    dc = (((unit >> 6) & 1) - core) & 1
    hf = unit & 1
    near = 4 + hf * 4 + (dz >> 1) * 2 + dc
    within = jnp.where(dz == 0, dc * 2 + hf, jnp.where(dz == 2, 12 + dc * 2 + hf, near))
    ncode[...] = (d2 * 4 + d1) * 16 + within

    def build(i):
        ids = i * 64 + lax.broadcasted_iota(I32, (64, queries), 0)
        acc = jnp.full((64, queries), -1, I32)
        for k in range(64):
            acc = jnp.where(ids == ncode[k : k + 1, :], nr[k : k + 1, :], acc)
        tsend[i * 4 : (i + 1) * 4] = acc.reshape(4, 16, queries)

    xq.wait()
    xp.wait()
    for c in range(n_in):
        wi_copy(c).wait()
        if c < n_out:
            wo_copy(c).start()
        s = slice(c * c_in, (c + 1) * c_in)
        h = jnp.dot(x[...], wi[:, s], preferred_element_type=F32)
        act[:, s] = jax.nn.gelu(h, approximate=True).astype(BF16)
        build(c)

    pl.semaphore_wait(barrier, 18)

    def back(p):
        return (4 - p // 4) % 4 * 4 + (4 - p % 4) % 4

    def request(p):
        return pltpu.make_async_remote_copy(
            src_ref=tsend.at[p], dst_ref=tin.at[back(p)], send_sem=rqs.at[p], recv_sem=rqr.at[back(p)],
            device_id=plane_dev(p % 4, p // 4), device_id_type=MESH,
        )

    def request_in(p):
        return pltpu.make_async_remote_copy(
            src_ref=tsend.at[p], dst_ref=tin.at[p], send_sem=rqs.at[p], recv_sem=rqr.at[p],
            device_id=plane_dev(p % 4, p // 4), device_id_type=MESH,
        )

    for p in range(1, 16):
        request(p).start()
    tin[0] = tsend[0]

    names = {}
    sent = []

    def copy(src, dst, name, dev):
        i = names.setdefault(name, len(names))
        return pltpu.make_async_remote_copy(
            src_ref=src, dst_ref=dst, send_sem=send.at[i], recv_sem=recv.at[i],
            device_id=dev, device_id_type=MESH,
        )

    def go(src, dst, name, dev):
        cp = copy(src, dst, name, dev)
        cp.start()
        sent.append(cp)

    def here(dst, name):
        copy(dst, dst, name, sib).wait_recv()

    def piece(row, slot, h):
        return qbuf.at[row, pl.ds(slot * 128, 128), pl.ds(h * c_out, c_out)]

    dev1 = {1: plane_dev(1, 0), 3: plane_dev(3, 0)}
    dev2 = {1: plane_dev(0, 1), 3: plane_dev(0, 3)}

    def spread1(h):
        for d in (1, 3):
            go(piece(0, 0, h), piece(0, 4 - d, h), ("one", 4 - d, h), dev1[d])

    def spread2(slot, h):
        for d in (1, 3):
            go(piece(0, slot, h), piece(4 - d, slot, h), ("two", 4 - d, slot, h), dev2[d])

    def pass1(h):
        d = 1 if h == 0 else 3
        go(piece(0, 4 - d, h), piece(0, 2, h), ("one", 2, h), dev1[d])

    def pass2(slot, h):
        d = 1 if h == 0 else 3
        go(piece(4 - d, slot, h), piece(2, slot, h), ("two", 2, slot, h), dev2[d])

    def here1(slot, h):
        here(piece(0, slot, h), ("one", slot, h))

    def here2(row, slot, h):
        here(piece(row, slot, h), ("two", row, slot, h))

    for h in range(n_out):
        wo_copy(h).wait()
        s = slice(h * c_out, (h + 1) * c_out)
        o = jnp.dot(act[0:queries, :], wo[:, s], preferred_element_type=F32)
        qbuf[0, 0:queries, s] = (x[0:queries, s].astype(F32) + o).astype(BF16)
        spread1(h)
        spread2(0, h)

    def slot_of(dz, dc, h):
        if dz == 0:
            return dc * 2 + h
        if dz == 2:
            return 12 + dc * 2 + h
        return 4 + h * 4 + dz // 2 * 2 + dc

    def block(dz, dc, h):
        return pbuf.at[pl.ds(slot_of(dz, dc, h) * 128, 128)]

    def go_p(src, dst, dev):
        go(block(*src), block(*dst), dst, dev)

    def here_p(*dst):
        here(block(*dst), dst)

    for h in range(2):
        r = slice(queries + h * 128, queries + (h + 1) * 128)
        for c in range(n_out):
            s = slice(c * c_out, (c + 1) * c_out)
            o = jnp.dot(act[r, :], wo[:, s], preferred_element_type=F32)
            pbuf[h * 128 : (h + 1) * 128, s] = (x[r, s].astype(F32) + o).astype(BF16)
        go_p((0, 0, h), (3, 0, h), dev_zp)
        go_p((0, 0, h), (1, 0, h), dev_zm)
        go_p((0, 0, h), (0, 1, h), sib)

    acc = jnp.zeros((64, queries), I32)
    for k in range(64):
        acc = jnp.where(ro[...] == k, ncode[k : k + 1, :], acc)
    code[...] = acc
    rows = lax.broadcasted_iota(I32, (128, 128), 0)
    lanes = lax.broadcasted_iota(I32, (128, 128), 1)
    dims = (((1,), (1,)), ((), ()))
    s_own = lax.dot_general(pbuf[0:128, :], qbuf[0, 0:128, :], dims, preferred_element_type=F32)
    pos = jnp.sum(jnp.where(rows == lanes, s_own, 0.0), axis=0, keepdims=True) * scale

    def score(row, q0, q1, u0, u1):
        s = lax.dot_general(
            pbuf[u0 * 128 : u1 * 128, :], qbuf[row, q0 * 128 : q1 * 128, :], dims, preferred_element_type=F32
        )
        for q in range(q0, q1):
            w = slice((q - q0) * 128, (q - q0 + 1) * 128)
            at = row * 4 + q
            for u in range(u0, u1):
                part = s[(u - u0) * 128 : (u - u0 + 1) * 128, w]
                hit = rows == tin[at, u : u + 1, :]
                hsend[at, u : u + 1, :] = jnp.sum(jnp.where(hit, part, 0.0), axis=0, keepdims=True)
            for k, u in ((0, 0), (1, 12)):
                if u0 <= u < u1:
                    part = s[(u - u0) * 128 : (u - u0 + 2) * 128, w]
                    top = jnp.max(part, axis=0, keepdims=True)
                    hsend[at, 16 + 2 * k : 17 + 2 * k, :] = top
                    hsend[at, 17 + 2 * k : 18 + 2 * k, :] = jnp.sum(
                        jnp.exp((part - top) * scale), axis=0, keepdims=True
                    )

    def answer(p):
        return pltpu.make_async_remote_copy(
            src_ref=hsend.at[p], dst_ref=hin.at[back(p)], send_sem=rts.at[p], recv_sem=rtr.at[back(p)],
            device_id=plane_dev(p % 4, p // 4), device_id_type=MESH,
        )

    def answer_in(p):
        return pltpu.make_async_remote_copy(
            src_ref=hsend.at[p], dst_ref=hin.at[p], send_sem=rts.at[p], recv_sem=rtr.at[p],
            device_id=plane_dev(p % 4, p // 4), device_id_type=MESH,
        )

    def answer_row(row):
        for slot in range(4):
            p = row * 4 + slot
            if p == 0:
                hin[0] = hsend[0]
            else:
                answer(p).start()

    here1(3, 0)
    pass1(0)
    spread2(3, 0)
    here1(1, 0)
    spread2(1, 0)
    here2(3, 0, 0)
    pass2(0, 0)
    here1(1, 1)
    pass1(1)
    spread2(1, 1)
    here1(3, 1)
    spread2(3, 1)
    here2(1, 0, 1)
    pass2(0, 1)
    for p in range(1, 16):
        request_in(p).wait_recv()
    here_p(0, 1, 0)
    here_p(0, 1, 1)
    score(0, 0, 2, 0, 4)
    here1(2, 0)
    spread2(2, 0)
    here1(2, 1)
    spread2(2, 1)
    here_p(3, 0, 0)
    go_p((3, 0, 0), (2, 0, 0), dev_zp)
    go_p((3, 0, 0), (3, 1, 0), sib)
    here_p(1, 0, 0)
    go_p((1, 0, 0), (1, 1, 0), sib)
    score(0, 2, 4, 0, 4)
    here_p(3, 1, 0)
    here_p(1, 1, 0)
    score(0, 0, 4, 4, 8)
    here2(3, 3, 0)
    pass2(3, 0)
    here2(3, 1, 0)
    pass2(1, 0)
    here2(1, 1, 1)
    pass2(1, 1)
    here2(1, 3, 1)
    pass2(3, 1)
    here_p(1, 0, 1)
    go_p((1, 0, 1), (2, 0, 1), dev_zm)
    go_p((1, 0, 1), (1, 1, 1), sib)
    here_p(3, 0, 1)
    go_p((3, 0, 1), (3, 1, 1), sib)
    here2(1, 0, 0)
    here2(1, 1, 0)
    score(1, 0, 2, 0, 8)
    here2(3, 0, 1)
    here2(3, 1, 1)
    score(3, 0, 2, 0, 8)
    here2(3, 2, 0)
    pass2(2, 0)
    here2(1, 2, 1)
    pass2(2, 1)
    here2(1, 2, 0)
    here2(1, 3, 0)
    score(1, 2, 4, 0, 8)
    here2(3, 2, 1)
    here2(3, 3, 1)
    score(3, 2, 4, 0, 8)
    here_p(1, 1, 1)
    here_p(3, 1, 1)
    for row in (0, 1, 3):
        score(row, 0, 4, 8, 12)
    here_p(2, 0, 0)
    go_p((2, 0, 0), (2, 1, 0), sib)
    here_p(2, 0, 1)
    go_p((2, 0, 1), (2, 1, 1), sib)
    for slot in (0, 1):
        here2(2, slot, 0)
        here2(2, slot, 1)
    score(2, 0, 2, 0, 8)
    score(2, 0, 2, 8, 12)
    here_p(2, 1, 0)
    here_p(2, 1, 1)
    for row in (1, 3):
        score(row, 0, 4, 12, 16)
        answer_row(row)
    score(2, 0, 2, 12, 16)
    for slot in (2, 3):
        here2(2, slot, 0)
        here2(2, slot, 1)
    score(2, 2, 4, 0, 8)
    score(2, 2, 4, 8, 16)
    answer_row(2)
    score(0, 0, 4, 12, 16)
    answer_row(0)

    ordered = jnp.zeros((64, queries), F32)
    for p in (4, 5, 6, 7, 12, 13, 14, 15, 8, 9, 10, 11, 0, 1, 2, 3):
        if p:
            answer_in(p).wait_recv()
        for j in range(16):
            ordered = jnp.where(code[...] == p * 16 + j, hin[p, j : j + 1, :], ordered)
    ordered = ordered * scale
    tops = jnp.concatenate([hin[:, 16, :], hin[:, 18, :]], axis=0) * scale
    totals = jnp.concatenate([hin[:, 17, :], hin[:, 19, :]], axis=0)
    top = jnp.maximum(jnp.max(tops, axis=0, keepdims=True), jnp.max(ordered, axis=0, keepdims=True))
    total = jnp.sum(totals * jnp.exp(tops - top), axis=0, keepdims=True)
    total = total + jnp.sum(jnp.exp(ordered - top), axis=0, keepdims=True)
    contrast_out[...] = jnp.log(total) + top - pos

    m, t = ordered, jnp.ones_like(ordered)
    for sh in (1, 2, 4, 8, 16, 32):
        m2 = jnp.concatenate([m[sh:], jnp.full((sh, queries), NEG_BIG, F32)], axis=0)
        t2 = jnp.concatenate([t[sh:], jnp.zeros((sh, queries), F32)], axis=0)
        mm = jnp.maximum(m, m2)
        t = t * jnp.exp(m - mm) + t2 * jnp.exp(m2 - mm)
        m = mm
    list_out[...] = jnp.mean(m + jnp.log(t) - ordered, axis=0, keepdims=True)

    for cp in sent:
        cp.wait_send()
    for p in range(1, 16):
        request(p).wait_send()
        answer(p).wait_send()


def body(query_hidden, passage_hidden, w_in, w_out, neg_unit, neg_row, rank_order):
    width, ff = w_in.shape
    anyspec = pl.BlockSpec(memory_space=pl.ANY)
    vmem = pl.BlockSpec(memory_space=pltpu.VMEM)
    dma = pltpu.SemaphoreType.DMA
    contrast, listwise = pl.pallas_call(
        kernel,
        out_shape=(jax.ShapeDtypeStruct((1, 128), F32), jax.ShapeDtypeStruct((1, 128), F32)),
        in_specs=[anyspec, anyspec, vmem, vmem, vmem, anyspec, anyspec],
        out_specs=(vmem, vmem),
        scratch_shapes=[
            pltpu.VMEM((width, ff), BF16),
            pltpu.VMEM((ff, width), BF16),
            pltpu.VMEM((384, width), BF16),
            pltpu.VMEM((384, ff), BF16),
            pltpu.VMEM((4, 512, width), BF16),
            pltpu.VMEM((2048, width), BF16),
            pltpu.VMEM((64, 128), I32),
            pltpu.VMEM((64, 128), I32),
            pltpu.VMEM((16, 16, 128), I32),
            pltpu.VMEM((16, 16, 128), I32),
            pltpu.VMEM((16, 24, 128), F32),
            pltpu.VMEM((16, 24, 128), F32),
            dma((6,)),
            dma((2,)),
            dma((44,)),
            dma((44,)),
            dma((16,)),
            dma((16,)),
            dma((16,)),
            dma((16,)),
        ],
        compiler_params=pltpu.CompilerParams(
            collective_id=0, has_side_effects=True, vmem_limit_bytes=56 * 1024 * 1024
        ),
        name="distill",
    )(query_hidden, passage_hidden, neg_unit.T, neg_row.T, rank_order.T, w_in, w_out)
    return contrast.reshape(128), listwise.reshape(128)


def solution(mesh):
    split = P(("group", "blk"), None)
    return jax.shard_map(
        body,
        mesh=mesh,
        in_specs=(split, split, P(), P(), split, split, split),
        out_specs=(P(("group", "blk")), P(("group", "blk"))),
        check_vma=False,
    )
```

time: 634 us -> 55.7 us (0.09)
  the two profiles are of different devices: /device:TPU:101 before, /device:TPU:1 now
where the time goes in v2:
time: 55.7 us; the launch traced here: 55.5 us
  Pallas kernels  52.6 us (94%)
  local copies, waits for them, and re-layouts  2.25 us (4%)
  between operations  0.64 us (1%)
    pallas_call x1, Pallas kernels, body(): pl.pallas_call(kernel, out_shape=(jax.ShapeDtypeStruct((1, 128), F32), ja...  52.6 us
    unnamed x2, local copies, waits for them, and re-layouts  2.25 us

profile of v2, /device:TPU:1, one launch (start us, length us, event | category | flops | bytes accessed | tf_op | source)
XLA Modules:
  0.0 55.5 jit_solution(13663808175279668718)
XLA Ops:
  0.6 52.6 %distill.1 = (f32[1,128]{1,0:T(1,128)}, f32[1,128]{1,0:T(1,128)}) custom-call(bf16[128,1024]{1,0:T(8,128)(2,1)} %qh.1, bf16[256,1024]{1,0:T(8,128)(2,1)} %ph.1, s32[64,128]{1,0:T(8,128)} %bitcast.5, s32[64,128]{1,0:T(8,128)} %bitcast.6, s32[64,128]{1,0:T(8,128)} %bitcast.7, bf16[1024,4096]{1,0:T(8,128)(2,1)} %wi_hbm.1, bf16[4096,1024]{1,0:T(8,128)(2,1)} %wo_hbm.1), custom_call_target="tpu_custom_call" | custom-call | tf_op jit(solution)/shard_map/distill/pallas_call | solution.py:379
  53.3 1.1 %copy.11 = f32[128]{0:T(128)} copy(f32[128]{0:T(128)} %bitcast.9) | data formatting | bytes 1024
  54.4 1.1 %copy.12 = f32[128]{0:T(128)} copy(f32[128]{0:T(128)} %bitcast.8) | data formatting | bytes 1024

commit v3 on v2

--- a/solution.py
+++ b/solution.py
@@ -15,9 +15,9 @@
 
 
 def kernel(
-    qh, ph, nu, nr, ro, wi_hbm, wo_hbm,
-    contrast_out, list_out,
-    wi, wo, x, act, qbuf, pbuf, ncode, code, tsend, tin, hsend, hin,
+    qh, ph, nu_in, nr_in, ro_in, wi_hbm, wo_hbm,
+    losses,
+    wi, wo, x, act, qbuf, pbuf, nu, nr, ro, ncode, code, tsend, tin, hsend, hin,
     wsem, xsem, send, recv, rqs, rqr, rts, rtr,
 ):
     width = x.shape[1]
@@ -48,29 +48,37 @@
 
     others = [(p % 4, p // 4) for p in range(1, 16)]
 
-    n_in, n_out = 4, 2
-    c_in, c_out = wi.shape[1] // n_in, wo.shape[1] // n_out
-
-    def wi_copy(i):
-        s = pl.ds(i * c_in, c_in)
-        return pltpu.make_async_copy(wi_hbm.at[:, s], wi.at[:, s], wsem.at[i])
-
-    def wo_copy(i):
-        s = pl.ds(i * c_out, c_out)
-        return pltpu.make_async_copy(wo_hbm.at[:, s], wo.at[:, s], wsem.at[n_in + i])
+    eighth = wi.shape[1] // 8
+    cuts = [0, eighth, 2 * eighth, 4 * eighth, 6 * eighth, 8 * eighth]
+    n_in, n_out = len(cuts) - 1, 2
+    c_out = wo.shape[1] // n_out
+
+    def w_copy(i):
+        if i < n_in:
+            s = pl.ds(cuts[i], cuts[i + 1] - cuts[i])
+            return pltpu.make_async_copy(wi_hbm.at[:, s], wi.at[:, s], wsem.at[i])
+        s = pl.ds((i - n_in) * c_out, c_out)
+        return pltpu.make_async_copy(wo_hbm.at[:, s], wo.at[:, s], wsem.at[i])
 
     xq = pltpu.make_async_copy(qh, x.at[pl.ds(0, queries)], xsem.at[0])
     xp = pltpu.make_async_copy(ph, x.at[pl.ds(queries, passages)], xsem.at[1])
     xq.start()
     xp.start()
-    for i in range(n_in):
-        wi_copy(i).start()
+    w_copy(0).start()
+    indices = [
+        pltpu.make_async_copy(src, dst, xsem.at[2 + i]) for i, (src, dst) in enumerate(((nu_in, nu), (nr_in, nr), (ro_in, ro)))
+    ]
+    for cp in indices:
+        cp.start()
+    w_copy(1).start()
 
     barrier = pltpu.get_barrier_semaphore()
     sib, dev_zp, dev_zm = column_dev(0, 1), column_dev(1, 0), column_dev(3, 0)
     for dev in [plane_dev(d1, d2) for d1, d2 in others] + [sib, dev_zp, dev_zm]:
         pl.semaphore_signal(barrier, inc=1, device_id=dev, device_id_type=MESH)
 
+    for cp in indices:
+        cp.wait()
     unit = nu[...]
     vx = (unit >> 2) & 3
     vy = (unit >> 4) & 3
@@ -79,7 +87,7 @@
     dz = (((unit >> 1) & 1) * 2 + ((unit >> 7) & 1) - z) & 3
     dc = (((unit >> 6) & 1) - core) & 1
     hf = unit & 1
-    near = 4 + hf * 4 + (dz >> 1) * 2 + dc
+    near = 4 + (hf ^ 1 ^ (dz >> 1)) * 4 + (dz >> 1) * 2 + dc
     within = jnp.where(dz == 0, dc * 2 + hf, jnp.where(dz == 2, 12 + dc * 2 + hf, near))
     ncode[...] = (d2 * 4 + d1) * 16 + within
 
@@ -93,15 +101,15 @@
     xq.wait()
     xp.wait()
     for c in range(n_in):
-        wi_copy(c).wait()
-        if c < n_out:
-            wo_copy(c).start()
-        s = slice(c * c_in, (c + 1) * c_in)
+        if c < 2:
+            build(2 * c)
+        w_copy(c).wait()
+        w_copy(c + 2).start()
+        s = slice(cuts[c], cuts[c + 1])
         h = jnp.dot(x[...], wi[:, s], preferred_element_type=F32)
         act[:, s] = jax.nn.gelu(h, approximate=True).astype(BF16)
-        build(c)
-
-    pl.semaphore_wait(barrier, 18)
+        if c < 2:
+            build(2 * c + 1)
 
     def back(p):
         return (4 - p // 4) % 4 * 4 + (4 - p % 4) % 4
@@ -118,6 +126,7 @@
             device_id=plane_dev(p % 4, p // 4), device_id_type=MESH,
         )
 
+    pl.semaphore_wait(barrier, 18)
     for p in range(1, 16):
         request(p).start()
     tin[0] = tsend[0]
@@ -169,19 +178,20 @@
         here(piece(row, slot, h), ("two", row, slot, h))
 
     for h in range(n_out):
-        wo_copy(h).wait()
+        w_copy(n_in + h).wait()
         s = slice(h * c_out, (h + 1) * c_out)
         o = jnp.dot(act[0:queries, :], wo[:, s], preferred_element_type=F32)
         qbuf[0, 0:queries, s] = (x[0:queries, s].astype(F32) + o).astype(BF16)
         spread1(h)
         spread2(0, h)
 
+
     def slot_of(dz, dc, h):
         if dz == 0:
             return dc * 2 + h
         if dz == 2:
             return 12 + dc * 2 + h
-        return 4 + h * 4 + dz // 2 * 2 + dc
+        return 4 + (h ^ 1 ^ (dz // 2)) * 4 + dz // 2 * 2 + dc
 
     def block(dz, dc, h):
         return pbuf.at[pl.ds(slot_of(dz, dc, h) * 128, 128)]
@@ -192,14 +202,13 @@
     def here_p(*dst):
         here(block(*dst), dst)
 
+    for c in range(n_out):
+        s = slice(c * c_out, (c + 1) * c_out)
+        o = jnp.dot(act[queries:, :], wo[:, s], preferred_element_type=F32)
+        pbuf[0:passages, s] = (x[queries:, s].astype(F32) + o).astype(BF16)
+    go_p((0, 0, 0), (3, 0, 0), dev_zp)
+    go_p((0, 0, 1), (1, 0, 1), dev_zm)
     for h in range(2):
-        r = slice(queries + h * 128, queries + (h + 1) * 128)
-        for c in range(n_out):
-            s = slice(c * c_out, (c + 1) * c_out)
-            o = jnp.dot(act[r, :], wo[:, s], preferred_element_type=F32)
-            pbuf[h * 128 : (h + 1) * 128, s] = (x[r, s].astype(F32) + o).astype(BF16)
-        go_p((0, 0, h), (3, 0, h), dev_zp)
-        go_p((0, 0, h), (1, 0, h), dev_zm)
         go_p((0, 0, h), (0, 1, h), sib)
 
     acc = jnp.zeros((64, queries), I32)
@@ -244,8 +253,8 @@
             device_id=plane_dev(p % 4, p // 4), device_id_type=MESH,
         )
 
-    def answer_row(row):
-        for slot in range(4):
+    def answer_row(row, slots):
+        for slot in slots:
             p = row * 4 + slot
             if p == 0:
                 hin[0] = hsend[0]
@@ -266,23 +275,23 @@
     spread2(3, 1)
     here2(1, 0, 1)
     pass2(0, 1)
+    go_p((0, 0, 1), (3, 0, 1), dev_zp)
+    go_p((0, 0, 0), (1, 0, 0), dev_zm)
+    here_p(3, 0, 0)
+    go_p((3, 0, 0), (3, 1, 0), sib)
+    here_p(1, 0, 1)
+    go_p((1, 0, 1), (1, 1, 1), sib)
+    here1(2, 0)
+    spread2(2, 0)
+    here1(2, 1)
+    spread2(2, 1)
     for p in range(1, 16):
         request_in(p).wait_recv()
     here_p(0, 1, 0)
     here_p(0, 1, 1)
-    score(0, 0, 2, 0, 4)
-    here1(2, 0)
-    spread2(2, 0)
-    here1(2, 1)
-    spread2(2, 1)
-    here_p(3, 0, 0)
-    go_p((3, 0, 0), (2, 0, 0), dev_zp)
-    go_p((3, 0, 0), (3, 1, 0), sib)
-    here_p(1, 0, 0)
-    go_p((1, 0, 0), (1, 1, 0), sib)
-    score(0, 2, 4, 0, 4)
+    score(0, 0, 4, 0, 4)
     here_p(3, 1, 0)
-    here_p(1, 1, 0)
+    here_p(1, 1, 1)
     score(0, 0, 4, 4, 8)
     here2(3, 3, 0)
     pass2(3, 0)
@@ -292,17 +301,18 @@
     pass2(1, 1)
     here2(1, 3, 1)
     pass2(3, 1)
-    here_p(1, 0, 1)
+    go_p((3, 0, 0), (2, 0, 0), dev_zp)
     go_p((1, 0, 1), (2, 0, 1), dev_zm)
-    go_p((1, 0, 1), (1, 1, 1), sib)
-    here_p(3, 0, 1)
-    go_p((3, 0, 1), (3, 1, 1), sib)
     here2(1, 0, 0)
     here2(1, 1, 0)
     score(1, 0, 2, 0, 8)
     here2(3, 0, 1)
     here2(3, 1, 1)
     score(3, 0, 2, 0, 8)
+    here_p(3, 0, 1)
+    go_p((3, 0, 1), (3, 1, 1), sib)
+    here_p(1, 0, 0)
+    go_p((1, 0, 0), (1, 1, 0), sib)
     here2(3, 2, 0)
     pass2(2, 0)
     here2(1, 2, 1)
@@ -313,8 +323,8 @@
     here2(3, 2, 1)
     here2(3, 3, 1)
     score(3, 2, 4, 0, 8)
-    here_p(1, 1, 1)
     here_p(3, 1, 1)
+    here_p(1, 1, 0)
     for row in (0, 1, 3):
         score(row, 0, 4, 8, 12)
     here_p(2, 0, 0)
@@ -328,21 +338,20 @@
     score(2, 0, 2, 8, 12)
     here_p(2, 1, 0)
     here_p(2, 1, 1)
-    for row in (1, 3):
-        score(row, 0, 4, 12, 16)
-        answer_row(row)
     score(2, 0, 2, 12, 16)
+    answer_row(2, (0, 1))
     for slot in (2, 3):
         here2(2, slot, 0)
         here2(2, slot, 1)
     score(2, 2, 4, 0, 8)
     score(2, 2, 4, 8, 16)
-    answer_row(2)
-    score(0, 0, 4, 12, 16)
-    answer_row(0)
+    answer_row(2, (2, 3))
+    for row in (1, 3, 0):
+        score(row, 0, 4, 12, 16)
+        answer_row(row, (0, 1, 2, 3))
 
     ordered = jnp.zeros((64, queries), F32)
-    for p in (4, 5, 6, 7, 12, 13, 14, 15, 8, 9, 10, 11, 0, 1, 2, 3):
+    for p in (8, 9, 10, 11, 4, 5, 6, 7, 12, 13, 14, 15, 0, 1, 2, 3):
         if p:
             answer_in(p).wait_recv()
         for j in range(16):
@@ -353,7 +362,7 @@
     top = jnp.maximum(jnp.max(tops, axis=0, keepdims=True), jnp.max(ordered, axis=0, keepdims=True))
     total = jnp.sum(totals * jnp.exp(tops - top), axis=0, keepdims=True)
     total = total + jnp.sum(jnp.exp(ordered - top), axis=0, keepdims=True)
-    contrast_out[...] = jnp.log(total) + top - pos
+    losses[0:1, :] = jnp.log(total) + top - pos
 
     m, t = ordered, jnp.ones_like(ordered)
     for sh in (1, 2, 4, 8, 16, 32):
@@ -362,7 +371,7 @@
         mm = jnp.maximum(m, m2)
         t = t * jnp.exp(m - mm) + t2 * jnp.exp(m2 - mm)
         m = mm
-    list_out[...] = jnp.mean(m + jnp.log(t) - ordered, axis=0, keepdims=True)
+    losses[1:2, :] = jnp.mean(m + jnp.log(t) - ordered, axis=0, keepdims=True)
 
     for cp in sent:
         cp.wait_send()
@@ -371,16 +380,21 @@
         answer(p).wait_send()
 
 
+def split_rows(both, first, second):
+    first[...] = both[0:1, :]
+    second[...] = both[1:2, :]
+
+
 def body(query_hidden, passage_hidden, w_in, w_out, neg_unit, neg_row, rank_order):
     width, ff = w_in.shape
     anyspec = pl.BlockSpec(memory_space=pl.ANY)
     vmem = pl.BlockSpec(memory_space=pltpu.VMEM)
     dma = pltpu.SemaphoreType.DMA
-    contrast, listwise = pl.pallas_call(
+    losses = pl.pallas_call(
         kernel,
-        out_shape=(jax.ShapeDtypeStruct((1, 128), F32), jax.ShapeDtypeStruct((1, 128), F32)),
-        in_specs=[anyspec, anyspec, vmem, vmem, vmem, anyspec, anyspec],
-        out_specs=(vmem, vmem),
+        out_shape=jax.ShapeDtypeStruct((8, 128), F32),
+        in_specs=[anyspec] * 7,
+        out_specs=vmem,
         scratch_shapes=[
             pltpu.VMEM((width, ff), BF16),
             pltpu.VMEM((ff, width), BF16),
@@ -390,12 +404,15 @@
             pltpu.VMEM((2048, width), BF16),
             pltpu.VMEM((64, 128), I32),
             pltpu.VMEM((64, 128), I32),
+            pltpu.VMEM((64, 128), I32),
+            pltpu.VMEM((64, 128), I32),
+            pltpu.VMEM((64, 128), I32),
             pltpu.VMEM((16, 16, 128), I32),
             pltpu.VMEM((16, 16, 128), I32),
             pltpu.VMEM((16, 24, 128), F32),
             pltpu.VMEM((16, 24, 128), F32),
-            dma((6,)),
-            dma((2,)),
+            dma((7,)),
+            dma((5,)),
             dma((44,)),
             dma((44,)),
             dma((16,)),
@@ -408,6 +425,13 @@
         ),
         name="distill",
     )(query_hidden, passage_hidden, neg_unit.T, neg_row.T, rank_order.T, w_in, w_out)
+    contrast, listwise = pl.pallas_call(
+        split_rows,
+        out_shape=(jax.ShapeDtypeStruct((1, 128), F32), jax.ShapeDtypeStruct((1, 128), F32)),
+        in_specs=[vmem],
+        out_specs=(vmem, vmem),
+        name="split_rows",
+    )(losses)
     return contrast.reshape(128), listwise.reshape(128)
 
 

time: 55.7 us -> 51.7 us (0.928)
  local copies, waits for them, and re-layouts: 2.25 us -> 0 us
  Pallas kernels: 52.6 us -> 50.9 us
    unnamed x2 -> x0, local copies, waits for them, and re-layouts: 2.25 us -> none
    pallas_call x1 -> x2, Pallas kernels: 52.6 us -> 50.9 us  [the longest x1 49.7 us: body(): pl.pallas_call(kernel, out_shape=jax.ShapeDtypeStruct((8, 128), F32), in_...]
where the time goes in v3:
time: 51.7 us; the launch traced here: 51.5 us
  Pallas kernels  50.9 us (98%)
  between operations  0.64 us (1%)
    pallas_call x1, Pallas kernels, body(): pl.pallas_call(kernel, out_shape=jax.ShapeDtypeStruct((8, 128), F32), in_...  49.7 us
    pallas_call x1, Pallas kernels, body(): pl.pallas_call(split_rows, out_shape=(jax.ShapeDtypeStruct((1, 128), F32)...  1.19 us

profile of v3, /device:TPU:1, one launch (start us, length us, event | category | flops | bytes accessed | tf_op | source)
XLA Modules:
  0.0 51.5 jit_solution(13361160242387510669)
XLA Ops:
  0.6 49.7 %distill.1.both = f32[8,128]{1,0:T(8,128)} custom-call(bf16[128,1024]{1,0:T(8,128)(2,1)} %qh.1, bf16[256,1024]{1,0:T(8,128)(2,1)} %ph.1, s32[64,128]{1,0:T(8,128)} %bitcast.5, s32[64,128]{1,0:T(8,128)} %bitcast.6, s32[64,128]{1,0:T(8,128)} %bitcast.7, bf16[1024,4096]{1,0:T(8,128)(2,1)} %wi_hbm.1, bf16[4096,1024]{1,0:T(8,128)(2,1)} %wo_hbm.1), custom_call_target="tpu_custom_call" | custom-call | tf_op jit(solution)/shard_map/distill/pallas_call | solution.py:393
  50.3 1.2 %split_rows.1 = (f32[1,128]{1,0:T(1,128)}, f32[1,128]{1,0:T(1,128)}) custom-call(f32[8,128]{1,0:T(8,128)} %distill.1.both), custom_call_target="tpu_custom_call" | custom-call | tf_op jit(solution)/shard_map/split_rows/pallas_call | solution.py:428

commit v4 on v3

--- a/solution.py
+++ b/solution.py
@@ -278,8 +278,10 @@
     go_p((0, 0, 1), (3, 0, 1), dev_zp)
     go_p((0, 0, 0), (1, 0, 0), dev_zm)
     here_p(3, 0, 0)
+    go_p((3, 0, 0), (2, 0, 0), dev_zp)
     go_p((3, 0, 0), (3, 1, 0), sib)
     here_p(1, 0, 1)
+    go_p((1, 0, 1), (2, 0, 1), dev_zm)
     go_p((1, 0, 1), (1, 1, 1), sib)
     here1(2, 0)
     spread2(2, 0)
@@ -301,8 +303,6 @@
     pass2(1, 1)
     here2(1, 3, 1)
     pass2(3, 1)
-    go_p((3, 0, 0), (2, 0, 0), dev_zp)
-    go_p((1, 0, 1), (2, 0, 1), dev_zm)
     here2(1, 0, 0)
     here2(1, 1, 0)
     score(1, 0, 2, 0, 8)
@@ -325,12 +325,13 @@
     score(3, 2, 4, 0, 8)
     here_p(3, 1, 1)
     here_p(1, 1, 0)
-    for row in (0, 1, 3):
-        score(row, 0, 4, 8, 12)
+    score(1, 0, 4, 8, 12)
     here_p(2, 0, 0)
     go_p((2, 0, 0), (2, 1, 0), sib)
     here_p(2, 0, 1)
     go_p((2, 0, 1), (2, 1, 1), sib)
+    for row in (0, 3):
+        score(row, 0, 4, 8, 12)
     for slot in (0, 1):
         here2(2, slot, 0)
         here2(2, slot, 1)

time: 51.7 us -> 50.8 us (0.983)
  Pallas kernels: 50.9 us -> 49.8 us
    pallas_call x1, Pallas kernels: 49.7 us -> 48.6 us  [body(): pl.pallas_call(kernel, out_shape=jax.ShapeDtypeStruct((8, 128), F32), in_...]
where the time goes in v4:
time: 50.8 us; the launch traced here: 50.5 us
  Pallas kernels  49.8 us (98%)
  between operations  0.64 us (1%)
    pallas_call x1, Pallas kernels, body(): pl.pallas_call(kernel, out_shape=jax.ShapeDtypeStruct((8, 128), F32), in_...  48.6 us
    pallas_call x1, Pallas kernels, body(): pl.pallas_call(split_rows, out_shape=(jax.ShapeDtypeStruct((1, 128), F32)...  1.19 us

profile of v4, /device:TPU:1, one launch (start us, length us, event | category | flops | bytes accessed | tf_op | source)
XLA Modules:
  0.0 50.5 jit_solution(8808377389708779497)
XLA Ops:
  0.6 48.6 %distill.1.both = f32[8,128]{1,0:T(8,128)} custom-call(bf16[128,1024]{1,0:T(8,128)(2,1)} %qh.1, bf16[256,1024]{1,0:T(8,128)(2,1)} %ph.1, s32[64,128]{1,0:T(8,128)} %bitcast.5, s32[64,128]{1,0:T(8,128)} %bitcast.6, s32[64,128]{1,0:T(8,128)} %bitcast.7, bf16[1024,4096]{1,0:T(8,128)(2,1)} %wi_hbm.1, bf16[4096,1024]{1,0:T(8,128)(2,1)} %wo_hbm.1), custom_call_target="tpu_custom_call" | custom-call | tf_op jit(solution)/shard_map/distill/pallas_call | solution.py:394
  49.3 1.2 %split_rows.1 = (f32[1,128]{1,0:T(1,128)}, f32[1,128]{1,0:T(1,128)}) custom-call(f32[8,128]{1,0:T(8,128)} %distill.1.both), custom_call_target="tpu_custom_call" | custom-call | tf_op jit(solution)/shard_map/split_rows/pallas_call | solution.py:429
